TPU v7x, 256 devices: a whole 4x4x8 slice. The times are simulated.
256 devices in a mesh: cfg: 2 (over x_lo), seq: 128 (over y, z, x_hi, core).
Axes of the slice: x: 4 (x_hi: 2, x_lo: 2; x = x_hi * 2 + x_lo), y: 4, z: 8, core: 2. Of those that a mesh axis runs over, the one named last changes fastest.
Arguments:
- coarse_hidden: bfloat16 [2, 256, 64, 2048], P('cfg', 'seq'), may hold values from -6 to 6
- coarse_modulation: float32 [2, 2, 2048], P('cfg'), may hold values from -3 to 3
- final_weight: bfloat16 [2048, 32], replicated, may hold values from -0.125 to 0.125
- coarse_latent: float32 [256, 2048], P('seq'), may hold values from -6 to 6
- step_index: int32 [1], replicated, may hold values from 0 to 49
- guide_index: int32 [1], replicated, may hold values from 0 to 4095
- guide_scales: float32 [4096], replicated, may hold values from 1.5 to 6
- upsample_weight: float32 [288, 32], replicated, may hold values from -0.375 to 0.375
- upsample_bias: float32 [32], replicated, may hold values from -3 to 3
- embed_weight: bfloat16 [32, 2048], replicated, may hold values from -1 to 1
- embed_bias: float32 [2048], replicated, may hold values from -3 to 3
- fine_modulation: float32 [3, 2048], replicated, may hold values from -3 to 3
- project_weight: bfloat16 [2048, 3072], P(('cfg', 'seq')), may hold values from -0.125 to 0.125
- query_gain: float32 [128], replicated, may hold values from 0.25 to 1.75
- key_gain: float32 [128], replicated, may hold values from 0.25 to 1.75
- text_keys: bfloat16 [256, 1024], replicated, may hold values from -6 to 6
- text_values: bfloat16 [256, 1024], replicated, may hold values from -6 to 6
- text_length: int32 [1], replicated, may hold values from 192 to 256
- output_weight: bfloat16 [1024, 2048], P(None, ('cfg', 'seq')), may hold values from -0.1875 to 0.1875
Outputs:
- guided_velocity: float32 [256, 2048], P('seq')
- fine_latent: float32 [256, 2, 4096], P('seq', 'cfg')
- fine_hidden: bfloat16 [256, 2, 128, 2048], P('seq', 'cfg')
All inputs are finite; a program needn't handle non-finite values.
Results may differ from a plain program's by a relative error of at most 0.0053.
Values may be sent and summed in bfloat16 or wider, within the bound.
A program may use at most 128 MiB of HBM per device.

v0:
```python
import jax
import jax.numpy as jnp
from jax import lax
from jax.sharding import PartitionSpec as P

HEADS = 8
STEPS = 50
epsilon = 1e-06
flow_shift = 5.0
highest = lax.Precision.HIGHEST


def from_partner(shard, axis, bit):
    return lax.ppermute(shard, axis, [(i, i ^ 1 << bit) for i in range(lax.axis_size(axis))])


def with_halo(block, sides, width):
    for axis, dim in sides:
        count = lax.axis_size(axis)
        forward = [(i, i + 1) for i in range(count - 1)]
        backward = [(target, source) for source, target in forward]
        low = lax.ppermute(
            lax.slice_in_dim(block, block.shape[dim] - width, None, axis=dim), axis, forward
        )
        high = lax.ppermute(lax.slice_in_dim(block, 0, width, axis=dim), axis, backward)
        block = jnp.concatenate([low, block, high], axis=dim)
    return block


def layer_norm(values):
    centred = values - jnp.mean(values, -1, keepdims=True)
    return centred * lax.rsqrt(jnp.mean(centred * centred, -1, keepdims=True) + epsilon)


def rms_heads(values, gain_vector, head_width):
    shaped = values.reshape(values.shape[0], -1, head_width)
    scaled = (
        shaped * lax.rsqrt(jnp.mean(shaped * shaped, -1, keepdims=True) + epsilon) * gain_vector
    )
    return scaled.reshape(values.shape[0], -1)


def sigma_at(step_value):
    fraction = 1.0 - step_value.astype(jnp.float32) / STEPS
    return flow_shift * fraction / (1.0 + (flow_shift - 1.0) * fraction)


def pick_scale(scale_table, slot_index):
    slots = jnp.arange(scale_table.shape[0], dtype=jnp.int32)
    return jnp.sum(jnp.where(slots == slot_index, scale_table, 0.0))


def attend(queries, image_keys, image_values, text_keys, text_values, image_mask, text_mask, heads):
    head_width = queries.shape[1] // heads
    score_scale = head_width ** (-0.5)
    dims = (((1,), (1,)), ((), ()))

    def one_head(head_index):
        column_start = head_index * head_width
        query_part = lax.dynamic_slice_in_dim(queries, column_start, head_width, 1)
        key_part = lax.dynamic_slice_in_dim(image_keys, column_start, head_width, 1)
        value_part = lax.dynamic_slice_in_dim(image_values, column_start, head_width, 1)
        text_key_part = lax.dynamic_slice_in_dim(text_keys, column_start, head_width, 1)
        text_value_part = lax.dynamic_slice_in_dim(text_values, column_start, head_width, 1)
        image_scores = (
            lax.dot_general(query_part, key_part, dims, preferred_element_type=jnp.float32)
            * score_scale
        )
        text_scores = (
            lax.dot_general(query_part, text_key_part, dims, preferred_element_type=jnp.float32)
            * score_scale
        )
        image_weights = jnp.where(image_mask, jnp.exp(image_scores), 0.0)
        text_weights = jnp.where(text_mask, jnp.exp(text_scores), 0.0)
        denominator = jnp.sum(image_weights, 1, keepdims=True) + jnp.sum(
            text_weights, 1, keepdims=True
        )
        image_weights = (image_weights / denominator).astype(jnp.bfloat16)
        text_weights = (text_weights / denominator).astype(jnp.bfloat16)
        return jnp.dot(image_weights, value_part, preferred_element_type=jnp.float32) + jnp.dot(
            text_weights, text_value_part, preferred_element_type=jnp.float32
        )

    stacked = lax.map(one_head, jnp.arange(heads, dtype=jnp.int32))
    return stacked.transpose(1, 0, 2).reshape(queries.shape[0], -1).astype(jnp.bfloat16)


def conv_rows(above, centre, below, upsample_weight, upsample_bias):
    tap_list = []
    for row_set in (above, centre, below):
        breadth = row_set.shape[1]
        padded = jnp.pad(row_set, ((0, 0), (1, 1), (0, 0)))
        for col_shift in range(3):
            tap_list.append(padded[:, col_shift : col_shift + breadth])
    patches = jnp.concatenate(tap_list, -1)
    flat_patches = patches.reshape(-1, patches.shape[-1])
    product = jnp.dot(flat_patches, upsample_weight, precision=highest).reshape(centre.shape)
    return product + upsample_bias + centre


def per_device(
    coarse_hidden,
    coarse_modulation,
    final_weight,
    coarse_latent,
    step_index,
    guide_index,
    guide_scales,
    upsample_weight,
    upsample_bias,
    embed_weight,
    embed_bias,
    fine_modulation,
    project_weight,
    query_gain,
    key_gain,
    text_keys,
    text_values,
    text_length,
    output_weight,
):
    row_count = coarse_hidden.shape[1]
    row_cells = coarse_hidden.shape[2]
    model_width = coarse_hidden.shape[3]
    channels = final_weight.shape[1]
    head_width = query_gain.shape[0]
    inner = project_weight.shape[1] // 3
    reach = max(row_count // 2, 1)
    branch = lax.axis_index("cfg")
    seq_index = lax.axis_index("seq")
    normed = layer_norm(coarse_hidden[0].astype(jnp.float32))
    modulated = (normed * (1.0 + coarse_modulation[0, 1]) + coarse_modulation[0, 0]).astype(
        jnp.bfloat16
    )
    velocity = jnp.dot(
        modulated.reshape(row_count * row_cells, model_width),
        final_weight,
        preferred_element_type=jnp.float32,
    ).reshape(row_count, row_cells * channels)
    partner = from_partner(velocity, "cfg", 0)
    conditional = jnp.where(branch == 0, velocity, partner)
    unconditional = jnp.where(branch == 0, partner, velocity)
    guidance = pick_scale(guide_scales, guide_index[0])
    guided = unconditional + guidance * (conditional - unconditional)
    stepped = coarse_latent + (sigma_at(step_index[0] + 1) - sigma_at(step_index[0])) * guided
    scale = 1.0 + fine_modulation[1]
    embed32 = embed_weight.astype(jnp.float32)
    embed_centred = embed32 - jnp.mean(embed32, -1, keepdims=True)
    bias_centred = embed_bias - jnp.mean(embed_bias)
    folded_left = jnp.concatenate(
        [embed_centred * scale, (bias_centred * scale)[None], fine_modulation[0][None]], 0
    )
    depth = project_weight.shape[0]
    device = branch * lax.axis_size("seq") + seq_index
    left_part = lax.dynamic_slice_in_dim(folded_left, device * depth, depth, 1)
    folded = lax.psum(
        jnp.dot(left_part, project_weight.astype(jnp.float32), precision=highest), ("cfg", "seq")
    )
    output_rows = lax.all_gather(output_weight.T, ("cfg", "seq"), axis=0, tiled=True)

    def embed_rows(grid_rows):
        grid_tokens = grid_rows.reshape(-1, channels).astype(jnp.bfloat16)
        centred = (
            jnp.dot(grid_tokens.astype(jnp.float32), embed_centred, precision=highest)
            + bias_centred
        )
        rstd = lax.rsqrt(jnp.mean(centred * centred, -1, keepdims=True) + epsilon)
        return (grid_tokens, rstd)

    def project(tokens_rstd, start, stop):
        tokens, rstd = tokens_rstd
        part = folded[:, start:stop]
        product = jnp.dot(tokens.astype(jnp.float32), part[:channels], precision=highest)
        return rstd * (product + part[channels]) + part[channels + 1]

    latent_grid = stepped.reshape(row_count, row_cells, channels)
    rim_width = reach + 1
    rimmed = with_halo(latent_grid, (("seq", 0),), rim_width)
    upsampled = jnp.repeat(jnp.repeat(rimmed, 2, 0), 2, 1)
    span = row_count + 2 * reach
    wide_grid = conv_rows(
        upsampled[1 : 1 + 2 * span],
        upsampled[2 : 2 + 2 * span],
        upsampled[3 : 3 + 2 * span],
        upsample_weight,
        upsample_bias,
    )
    grouped = wide_grid.reshape(span, 2, 2 * row_cells, channels)
    fine_grid = lax.dynamic_index_in_dim(
        grouped[reach : reach + row_count], branch, 1, keepdims=False
    )
    own = embed_rows(fine_grid)
    fine_state = jnp.dot(own[0], embed_weight, preferred_element_type=jnp.float32) + embed_bias
    around = embed_rows(wide_grid)
    token_count = own[0].shape[0]
    query_sum = project(own, 0, inner)
    key_sum = project(around, inner, 2 * inner)
    value_sum = project(around, 2 * inner, 3 * inner)
    queries = rms_heads(query_sum, query_gain, head_width).astype(jnp.bfloat16)
    keys = rms_heads(key_sum, key_gain, head_width).astype(jnp.bfloat16)
    values = value_sum.astype(jnp.bfloat16)
    image_keys, image_values = (keys, values)
    normed_text_keys = rms_heads(text_keys.astype(jnp.float32), key_gain, head_width).astype(
        jnp.bfloat16
    )
    key_count = image_keys.shape[0]
    query_rows = jnp.arange(token_count, dtype=jnp.int32) // (2 * row_cells)
    key_rows = jnp.arange(key_count, dtype=jnp.int32) // (4 * row_cells)
    distance = key_rows[None, :] - query_rows[:, None]
    global_rows = seq_index * row_count + key_rows - reach
    row_valid = (global_rows >= 0) & (global_rows < row_count * lax.axis_size("seq"))
    image_mask = (distance >= 0) & (distance <= 2 * reach) & row_valid[None, :]
    text_mask = (jnp.arange(text_keys.shape[0], dtype=jnp.int32) < text_length[0])[None, :]
    attended = attend(
        queries,
        image_keys,
        image_values,
        normed_text_keys,
        text_values,
        image_mask,
        text_mask,
        HEADS,
    )
    output_part = lax.dot_general(
        attended, output_rows, (((1,), (1,)), ((), ())), preferred_element_type=jnp.float32
    )
    fine_hidden = (fine_state + fine_modulation[2] * output_part).astype(jnp.bfloat16)
    fine_hidden = fine_hidden.reshape(row_count, 1, 2 * row_cells, model_width)
    fine_latent = fine_grid.reshape(row_count, 1, 2 * row_cells * channels)
    return (guided, fine_latent, fine_hidden)


def solution(mesh):
    placed = (
        P("cfg", "seq", None, None),
        P("cfg", None, None),
        P(),
        P("seq", None),
        P(),
        P(),
        P(),
        P(),
        P(),
        P(),
        P(),
        P(),
        P(("cfg", "seq"), None),
        P(),
        P(),
        P(),
        P(),
        P(),
        P(None, ("cfg", "seq")),
    )
    return jax.shard_map(
        per_device,
        mesh=mesh,
        in_specs=placed,
        out_specs=(P("seq", None), P("seq", "cfg", None), P("seq", "cfg", None, None)),
        check_vma=False,
    )
```

profile of v0, /device:TPU:32, one launch (start us, length us, event | category | flops | bytes accessed | tf_op | source)
XLA Modules:
  0.0 696.4 jit_solution(8204464123050728577)
XLA Ops:
  7.3 1.5 fusion.84
  10.8 1.3 reduce_sum.112
  13.5 2.0 fusion.65
  17.0 1.6 collective-permute-start
  23.5 1.3 multiply_add_fusion.1
  24.9 1.9 collective-permute-start.1
  27.4 6.0 collective-permute-start.2
  33.5 1.8 collective-permute-done.2
  39.3 1.2 fusion.28
  40.4 4.5 multiply_reduce_fusion
  45.0 223.4 %all-reduce.5.cloned.1.call-done = f32[34,3072]{1,0:T(8,128)} async-done(((f32[34,3072]{1,0:T(8,128)}), f32[34,3072]{1,0:T(8,128)}) %all-reduce.5.cloned.1.call-update) | async-done | bytes 417808 | tf_op jit(solution)/shard_map/psum | solution.py:156
  269.3 1.6 fusion.30
  271.7 3.4 bitcast_reduce_fusion
  275.9 1.1 fusion.23
  277.0 4.4 add_convert_fusion
  281.9 58.2 %while.11 = (s32[]{:T(128)}, bf16[8,256,128]{1,2,0:T(8,128)(2,1)}, s32[8]{0:T(128)}, bf16[256,1024]{1,0:T(8,128)(2,1)S(1)}, bf16[1024,1024]{0,1:T(8,128)(2,1)S(1...) while((s32[]{:T(128)}, bf16[8,256,128]{1,2,0:T(8,128)(2,1)}, ...), condition=%wide.region_14.15_spmd.clone, body=%wide.region_11.14_spmd.clone.sunk | while | flops 170786816 | bytes 4014055 | solution.py:84
  281.9 1.2 dynamic_slice.86
  284.7 1.3 fusion.102
  286.0 1.1 fusion.103
  287.1 1.3 fusion.104
  289.2 1.2 dynamic_slice.86
  291.9 1.3 fusion.102
  293.3 1.1 fusion.103
  294.3 1.3 fusion.104
  296.4 1.2 dynamic_slice.86
  299.2 1.3 fusion.102
  301.6 1.3 fusion.104
  303.7 1.2 dynamic_slice.86
  306.5 1.3 fusion.102
  308.9 1.3 fusion.104
  311.0 1.2 dynamic_slice.86
  313.8 1.3 fusion.102
  315.1 1.1 fusion.103
  316.2 1.3 fusion.104
  318.3 1.2 dynamic_slice.86
  321.0 1.3 fusion.102
  323.4 1.3 fusion.104
  325.5 1.2 dynamic_slice.86
  328.3 1.3 fusion.102
  329.6 1.1 fusion.103
  330.7 1.3 fusion.104
  332.8 1.2 dynamic_slice.86
  335.6 1.3 fusion.102
  336.9 1.1 fusion.103
  338.0 1.3 fusion.104
  340.1 344.3 %all-gather.2.cloned.1.call-done = bf16[2048,1024]{1,0:T(8,128)(2,1)} async-done(((bf16[8,1024]{1,0:T(8,128)(2,1)}), bf16[2048,1024]{1,0:T(8,128)(2,1)}) %all-gather.2.cloned.1.call-update) | async-done | bytes 4194320 | tf_op jit(solution)/shard_map/all_gather | solution.py:159
  684.4 3.6 convolution_multiply_fusion.2
  688.1 1.4 fusion.27
  (153 shorter events, 31.5 us)
Async XLA Ops:
  7.2 9.5 %copy-start = (bf16[2048,32]{0,1:T(8,128)(2,1)S(1)}, bf16[2048,32]{0,1:T(8,128)(2,1)}, u32[]{:S(2)}) copy-start(bf16[2048,32]{0,1:T(8,128)(2,1)} %param.23) | copy-start | bytes 393220
  7.2 8.4 %copy-start.1 = (bf16[1,2,64,2048]{3,2,1,0:T(8,128)(2,1)S(1)}, bf16[1,2,64,2048]{3,2,1,0:T(8,128)(2,1)}, u32[]{:S(2)}) copy-start(bf16[1,2,64,2048]{3,2,1,0:T(8,128)(2,1)} %param.21) | copy-start | bytes 1572868
  7.2 8.9 %copy-start.8 = (f32[1,2,2048]{2,1,0:T(2,128)S(1)}, f32[1,2,2048]{2,1,0:T(2,128)}, u32[]{:S(2)}) copy-start(f32[1,2,2048]{2,1,0:T(2,128)} %param.22) | copy-start | bytes 49156
  7.2 261.2 %all-reduce.5.cloned.1.call-start = ((), (), s32[]{:S(2)}) async-start(), calls=%async_computation | async-start | bytes 983040 | tf_op jit(solution)/shard_map/psum | solution.py:156
  13.4 6.4 copy-start.12
  13.5 6.5 copy-start.13
  13.5 6.5 copy-start.2
  15.5 668.9 %all-gather.2.cloned.1.call-start = ((), (), s32[]{:S(2)}) async-start(), calls=%async_computation.1 | async-start | bytes 4210688 | tf_op jit(solution)/shard_map/all_gather | solution.py:159
  17.0 6.4 collective-permute-start
  20.1 0.8 copy-start.9
  20.6 2.9 copy-start.10
  24.9 8.6 %collective-permute-start.1 = (f32[2,64,32]{2,1,0:T(8,128)S(1)}, f32[2,64,32]{2,1,0:T(8,128)S(1)}, u32[]{:S(2)}, u32[]{:S(2)}) collective-permute-start(f32[2,64,32]{2,1,0:T(8,128)S(1)} %reshape.230), channel_id=1, source_target_pairs={{0,1},{1,2},{2,3},{3,4},{4,5},{5,6},{6,7},{7,8},{8,9},{9,10},{10,1... | collective-permute-start | bytes 49160 | tf_op jit(solution)/shard_map/ppermute | solution.py:22
  27.4 7.9 %collective-permute-start.2 = (f32[2,64,32]{2,1,0:T(8,128)S(1)}, f32[2,64,32]{2,1,0:T(8,128)S(1)}, u32[]{:S(2)}, u32[]{:S(2)}) collective-permute-start(f32[2,64,32]{2,1,0:T(8,128)S(1)} %reshape.230), channel_id=1, source_target_pairs={{1,0},{2,1},{3,2},{4,3},{5,4},{6,5},{7,6},{8,7},{9,8},{10,9},{11,1... | collective-permute-start | bytes 49160 | tf_op jit(solution)/shard_map/ppermute | solution.py:25
  36.3 1.1 copy-start.7
  36.3 1.1 copy-start.11
  36.9 2.3 copy-start.3
  38.4 233.4 %copy-start.5 = (bf16[8,4,8,128]{3,2,1,0:T(8,128)(2,1)}, bf16[8,4,8,128]{3,2,1,0:T(8,128)(2,1)S(1)}, u32[]{:S(2)}) copy-start(bf16[8,4,8,128]{3,2,1,0:T(8,128)(2,1)S(1)} %convert_bitcast_fusion) | copy-start | bytes 196612
  275.9 1.1 copy-start.6
  684.4 3.6 copy-start.4
Sparse Core Ops, SparseCore 0:
  15.6 252.6 all-reduce.4
  270.3 414.1 all-gather.1
where the time goes:
time: 698 us; the launch traced here: 696 us
  waiting for transfers between devices  570 us (82%)
  matrix products  55 us (8%)
  local copies, waits for them, and re-layouts  21.8 us (3%)
  other arithmetic  18.2 us (3%)
  between operations  16.7 us (2%)
  starting transfers between devices  9.61 us (1%)
    all_gather x1, waiting for transfers between devices, per_device(): lax.all_gather(output_weight.T, ('cfg', 'seq'), axis=0, tiled=True)  344 us
    psum x1, waiting for transfers between devices, per_device(): lax.psum(jnp.dot(left_part, project_weight.astype(jnp.float32), precision...  223 us
  transfers between devices with their start and end apart: 5, of which 3 were waited for; matrix products, arithmetic and copies ran while one was open for 12% of the time, Pallas kernels for 0%

commit v1 on v0

--- a/solution.py
+++ b/solution.py
@@ -154,7 +154,8 @@
     device = branch * lax.axis_size("seq") + seq_index
     left_part = lax.dynamic_slice_in_dim(folded_left, device * depth, depth, 1)
     folded = lax.psum(
-        jnp.dot(left_part, project_weight.astype(jnp.float32), precision=highest), ("cfg", "seq")
+        lax.psum(jnp.dot(left_part, project_weight.astype(jnp.float32), precision=highest), "seq"),
+        "cfg",
     )
     output_rows = lax.all_gather(output_weight.T, ("cfg", "seq"), axis=0, tiled=True)
 

time: 698 us -> 1620 us (2.32)
  waiting for transfers between devices: 570 us -> 1490 us
    psum x1, waiting for transfers between devices: 223 us -> 1170 us  [per_device(): lax.psum(jnp.dot(left_part, project_weight.astype(jnp.float32), precision...]
    all_gather x1, waiting for transfers between devices: 344 us -> 309 us  [per_device(): lax.all_gather(output_weight.T, ('cfg', 'seq'), axis=0, tiled=True)]
  transfers between devices with their start and end apart: 5 -> 6, of which waited for: 3 -> 4; matrix products, arithmetic and copies ran while one was open for 12% -> 5% of each run, Pallas kernels for 0% -> 0%
where the time goes in v1:
time: 1620 us
  waiting for transfers between devices  1490 us (92%)
  matrix products  55 us (3%)
  local copies, waits for them, and re-layouts  21.8 us (1%)
  other arithmetic  18.2 us (1%)
  between operations  18.2 us (1%)
    psum x1, waiting for transfers between devices, per_device(): lax.psum(jnp.dot(left_part, project_weight.astype(jnp.float32), precision...  1170 us
    all_gather x1, waiting for transfers between devices, per_device(): lax.all_gather(output_weight.T, ('cfg', 'seq'), axis=0, tiled=True)  309 us
  transfers between devices with their start and end apart: 6, of which 4 were waited for; matrix products, arithmetic and copies ran while one was open for 5% of the time, Pallas kernels for 0%

profile of v1, /device:TPU:32, one launch (start us, length us, event | category | flops | bytes accessed | tf_op | source)
XLA Modules:
  0.0 1622.0 jit_solution(9581043041494488295)
XLA Ops:
  8.1 1.5 fusion.84
  11.6 1.3 reduce_sum.112
  14.3 2.0 fusion.65
  17.0 1168.2 %all-reduce.6.cloned.1.call-done = f32[34,3072]{1,0:T(8,128)} async-done(((f32[34,3072]{1,0:T(8,128)}), f32[34,3072]{1,0:T(8,128)}) %all-reduce.6.cloned.1.call-update) | async-done | bytes 417808 | tf_op jit(solution)/shard_map/psum | solution.py:157
  1186.1 1.3 collective-permute-start
  1192.3 1.3 multiply_add_fusion.1
  1193.7 1.9 collective-permute-start.1
  1196.2 6.3 collective-permute-start.2
  1202.5 1.8 collective-permute-done.2
  1208.3 1.2 fusion.28
  1209.5 4.5 multiply_reduce_fusion
  1214.1 14.8 all-reduce.8.cloned.1.call-done
  1229.8 1.6 fusion.30
  1232.2 3.4 bitcast_reduce_fusion
  1236.4 1.1 fusion.23
  1237.5 4.4 add_convert_fusion
  1242.4 58.2 %while.11 = (s32[]{:T(128)}, bf16[8,256,128]{1,2,0:T(8,128)(2,1)}, s32[8]{0:T(128)}, bf16[256,1024]{1,0:T(8,128)(2,1)S(1)}, bf16[1024,1024]{0,1:T(8,128)(2,1)S(1...) while((s32[]{:T(128)}, bf16[8,256,128]{1,2,0:T(8,128)(2,1)}, ...), condition=%wide.region_15.16_spmd.clone, body=%wide.region_12.15_spmd.clone.sunk | while | flops 170786816 | bytes 4014055 | solution.py:84
  1242.4 1.2 dynamic_slice.86
  1245.2 1.3 fusion.102
  1247.6 1.3 fusion.104
  1249.7 1.2 dynamic_slice.86
  1252.5 1.3 fusion.102
  1253.8 1.1 fusion.103
  1254.9 1.3 fusion.104
  1257.0 1.2 dynamic_slice.86
  1259.7 1.3 fusion.102
  1262.1 1.3 fusion.104
  1264.2 1.2 dynamic_slice.86
  1267.0 1.3 fusion.102
  1269.4 1.3 fusion.104
  1271.5 1.2 dynamic_slice.86
  1274.3 1.3 fusion.102
  1275.6 1.1 fusion.103
  1276.7 1.3 fusion.104
  1278.8 1.2 dynamic_slice.86
  1281.6 1.3 fusion.102
  1282.9 1.1 fusion.103
  1284.0 1.3 fusion.104
  1286.1 1.2 dynamic_slice.86
  1288.8 1.3 fusion.102
  1291.3 1.3 fusion.104
  1293.3 1.2 dynamic_slice.86
  1296.1 1.3 fusion.102
  1297.4 1.1 fusion.103
  1298.5 1.3 fusion.104
  1300.6 308.8 %all-gather.2.cloned.1.call-done = bf16[2048,1024]{1,0:T(8,128)(2,1)} async-done(((bf16[8,1024]{1,0:T(8,128)(2,1)}), bf16[2048,1024]{1,0:T(8,128)(2,1)}) %all-gather.2.cloned.1.call-update) | async-done | bytes 4194320 | tf_op jit(solution)/shard_map/all_gather | solution.py:160
  1609.5 3.6 convolution_multiply_fusion.2
  1613.1 1.4 fusion.27
  (156 shorter events, 32.6 us)
Async XLA Ops:
  8.0 1177.7 %copy-start = (bf16[2048,32]{0,1:T(8,128)(2,1)S(1)}, bf16[2048,32]{0,1:T(8,128)(2,1)}, u32[]{:S(2)}) copy-start(bf16[2048,32]{0,1:T(8,128)(2,1)} %param.23) | copy-start | bytes 393220
  8.0 8.3 copy-start.1
  8.0 9.0 copy-start.8
  8.0 1177.2 %all-reduce.6.cloned.1.call-start = ((), (), s32[]{:S(2)}) async-start(), calls=%async_computation | async-start | bytes 983040 | tf_op jit(solution)/shard_map/psum | solution.py:157
  16.3 1172.4 %copy-start.12 = (f32[128]{0:T(128)S(1)}, f32[128]{0:T(128)}, u32[]{:S(2)}) copy-start(f32[128]{0:T(128)} %param.34) | copy-start | bytes 1540
  16.3 1172.4 %copy-start.13 = (f32[128]{0:T(128)S(1)}, f32[128]{0:T(128)}, u32[]{:S(2)}) copy-start(f32[128]{0:T(128)} %param.35) | copy-start | bytes 1540
  16.3 1172.5 %copy-start.2 = (bf16[256,1024]{1,0:T(8,128)(2,1)S(1)}, bf16[256,1024]{1,0:T(8,128)(2,1)}, u32[]{:S(2)}) copy-start(bf16[256,1024]{1,0:T(8,128)(2,1)} %param.36) | copy-start | bytes 1572868
  16.3 1212.6 %all-reduce.8.cloned.1.call-start = ((), (), s32[]{:S(2)}) async-start(), calls=%async_computation.1 | async-start | bytes 983040 | tf_op jit(solution)/shard_map/psum | solution.py:156
  1185.3 424.2 %all-gather.2.cloned.1.call-start = ((), (), s32[]{:S(2)}) async-start(), calls=%async_computation.2 | async-start | bytes 4210688 | tf_op jit(solution)/shard_map/all_gather | solution.py:160
  1186.1 6.2 collective-permute-start
  1188.8 0.8 copy-start.9
  1189.4 2.9 copy-start.10
  1193.7 8.8 collective-permute-start.1
  1196.2 8.2 collective-permute-start.2
  1205.4 1.1 copy-start.7
  1205.4 1.1 copy-start.11
  1206.0 2.3 copy-start.3
  1207.4 24.8 %copy-start.5 = (bf16[8,4,8,128]{3,2,1,0:T(8,128)(2,1)}, bf16[8,4,8,128]{3,2,1,0:T(8,128)(2,1)S(1)}, u32[]{:S(2)}) copy-start(bf16[8,4,8,128]{3,2,1,0:T(8,128)(2,1)S(1)} %convert_bitcast_fusion) | copy-start | bytes 196612
  1236.4 1.1 copy-start.6
  1609.5 3.6 copy-start.4
Sparse Core Ops, SparseCore 0:
  16.4 1168.7 all-reduce.5
  1188.0 40.8 all-reduce.7
Sparse Core Ops, SparseCore 1:
  1187.8 421.6 all-gather.1
